TPU v7x, 512 devices: a whole 4x4x16 slice. The times are simulated.
512 devices in a mesh: tm: 16 (over y_lo, x, core), chan: 32 (over z, y_hi).
Axes of the slice: x: 4, y: 4 (y_hi: 2, y_lo: 2; y = y_hi * 2 + y_lo), z: 16, core: 2. Of those that a mesh axis runs over, the one named last changes fastest.
Arguments:
- record: float32 [16384, 4096], P('tm', 'chan'), may hold values from -6 to 6
- cuts: int32 [16, 1024], P('tm'), may hold values from 0 to 2048, as said below
Outputs:
- filtered: float32 [16384, 4096], P('tm', 'chan')
Inputs may be any that keep to these rules, and one draw needn't show every extreme that they name: cuts[w, b] is the largest wavenumber magnitude kept in window w at frequency band b.
All inputs are finite; a program needn't handle non-finite values.
Results may differ from a plain program's by a relative error of at most 0.0003.
Values sent between devices are 32-bit elements; how exact they have to be, the bound alone decides.
A program may use at most 64 MiB of HBM per device.

v0:
```python
import functools
import math

import jax
import jax.numpy as jnp
import ml_dtypes
import numpy as np
from jax import lax
from jax.experimental import pallas as pl
from jax.experimental.pallas import tpu as pltpu
from jax.sharding import PartitionSpec as P

WIN = 2048
HOP = WIN // 2
RIM = HOP // 2
NCH = 4096
GROUPS = 32
LANES = 128
RING = 16
PARTS = 17
SUB = 1
CHUNKS = 2 * SUB
ROWS = 32 // SUB
BLOCK = 256
SPAN = HOP // SUB
FAR = 17
MESH_ID = pl.DeviceIdType.MESH


def split_bf16(table):
    high = table.astype(np.float32).astype(ml_dtypes.bfloat16)
    low = (table - high.astype(np.float64)).astype(ml_dtypes.bfloat16)
    return np.stack([high, low])


def cas(angle):
    return np.cos(angle) + np.sin(angle)


@functools.cache
def tables():
    index = np.arange(HOP)
    even = cas(2.0 * np.pi / HOP * (np.outer(index, index) % HOP))
    odd_index = 2 * index + 1
    odd = cas(2.0 * np.pi / (2 * WIN) * (np.outer(odd_index, odd_index) % (2 * WIN)))
    time = np.concatenate([split_bf16(even), split_bf16(odd)])
    taper = np.sin(np.pi / WIN * np.arange(WIN)) ** 2
    taper = np.repeat(taper[:, None], LANES, axis=1).astype(np.float32)
    lane = np.arange(LANES)
    angle = 2.0 * np.pi / LANES * (np.outer(lane, lane) % LANES)
    cosine, sine = np.cos(angle), np.sin(angle)
    forward = np.block([[cosine, -sine], [sine, cosine]])
    inverse = np.block([[cosine, sine], [-sine, cosine]])
    chan = np.concatenate([split_bf16(forward), split_bf16(inverse)])
    angle = 2.0 * np.pi / NCH * np.outer(np.arange(PARTS), lane)
    twist = np.stack([np.cos(angle), np.sin(angle)]).astype(np.float32)
    twist = np.repeat(twist[:, :, None, :], 8, axis=2)
    wave = np.arange(PARTS)[:, None] + GROUPS * lane[None, :]
    wave = np.minimum(wave, NCH - wave)
    wave = np.concatenate([wave, wave], axis=1).astype(np.int32)
    wave = np.repeat(wave[:, None, :], 8, axis=1)
    return time, taper, chan, twist, wave


def real_dft(x):
    n = len(x)
    if n == 1:
        return [(x[0], None)]
    if n == 2:
        return [(x[0] + x[1], None), (x[0] - x[1], None)]
    even = real_dft(x[0::2])
    odd = real_dft(x[1::2])
    half = n // 2
    out = [None] * (half + 1)
    out[0] = (even[0][0] + odd[0][0], None)
    out[half] = (even[0][0] - odd[0][0], None)
    for k in range(1, half // 2 + 1):
        e_re, e_im = even[k]
        o_re, o_im = odd[k]
        if 2 * k == half:
            out[k] = (e_re, -o_re)
            continue
        c, s = math.cos(2.0 * math.pi * k / n), math.sin(2.0 * math.pi * k / n)
        t_re = c * o_re + s * o_im
        t_im = c * o_im - s * o_re
        out[k] = (e_re + t_re, e_im + t_im)
        out[half - k] = (e_re - t_re, t_im - e_im)
    return out


def real_inverse(spec):
    half = len(spec) - 1
    n = 2 * half
    first, last = spec[0][0], spec[half][0]
    if n == 2:
        return [first + last, first - last]
    even = [None] * (half // 2 + 1)
    odd = [None] * (half // 2 + 1)
    even[0] = (first + last, None)
    odd[0] = (first - last, None)
    for k in range(1, half // 2 + 1):
        a_re, a_im = spec[k]
        if 2 * k == half:
            even[k] = (2.0 * a_re, None)
            odd[k] = (-2.0 * a_im, None)
            continue
        b_re, b_im = spec[half - k]
        even[k] = (a_re + b_re, a_im - b_im)
        d_re, d_im = a_re - b_re, a_im + b_im
        c, s = math.cos(2.0 * math.pi * k / n), math.sin(2.0 * math.pi * k / n)
        odd[k] = (c * d_re - s * d_im, c * d_im + s * d_re)
    y_even = real_inverse(even)
    y_odd = real_inverse(odd)
    out = []
    for a, b in zip(y_even, y_odd):
        out += [a, b]
    return out


def dot(a, b):
    return jnp.dot(a, b, preferred_element_type=jnp.float32)


def halves(x):
    high = x.astype(jnp.bfloat16)
    low = (x - high.astype(jnp.float32)).astype(jnp.bfloat16)
    return high, low


def table_product(x, high_table, low_table):
    high, low = halves(x)
    return dot(high, high_table) + dot(high, low_table) + dot(low, high_table)


def peer_of(step, zed, side):
    there = (zed + 7 * (step // 2)) % RING
    return 2 * there + (side + step) % 2


def body(
    record_hbm, cuts_hbm, time_hbm, taper_hbm, chan_hbm, twist_hbm, wave_hbm,
    out,
    record, cuts, time, taper, chan, twist, wave, below, above, pair, rhs, send, recv, spec, turned, back, part,
    part_odd, low_in, high_in, go_hold, ret_hold,
    load_sem, halo_send, halo_recv, spill_send, spill_recv, go_send, go_recv, ret_send, ret_recv,
    hold_recv, hold_send,
):
    me = lax.axis_index("chan")
    tm = lax.axis_index("tm")
    count = 16
    zed, side = me // 2, me % 2
    up = (tm + 1) % count
    down = (tm + count - 1) % count

    loads = [
        pltpu.make_async_copy(record_hbm, record, load_sem.at[0]),
        pltpu.make_async_copy(taper_hbm, taper, load_sem.at[1]),
    ]
    for i in range(4):
        loads.append(pltpu.make_async_copy(time_hbm.at[i], time.at[i], load_sem.at[2 + i]))
    loads += [
        pltpu.make_async_copy(cuts_hbm, cuts, load_sem.at[6]),
        pltpu.make_async_copy(chan_hbm, chan, load_sem.at[7]),
        pltpu.make_async_copy(twist_hbm, twist, load_sem.at[8]),
        pltpu.make_async_copy(wave_hbm, wave, load_sem.at[9]),
    ]
    for load in loads:
        load.start()

    barrier = pltpu.get_barrier_semaphore()
    for other in (up, down):
        pl.semaphore_signal(barrier, inc=1, device_id={"tm": other}, device_id_type=MESH_ID)

    @pl.loop(1, GROUPS)
    def _(step):
        pl.semaphore_signal(
            barrier, inc=1, device_id={"chan": peer_of(step, zed, side)}, device_id_type=MESH_ID
        )

    pl.semaphore_wait(barrier, GROUPS + 1)

    halos = [
        pltpu.make_async_remote_copy(
            src_ref=record_hbm.at[pl.ds(RIM, RIM)], dst_ref=below,
            send_sem=halo_send.at[0], recv_sem=halo_recv.at[0],
            device_id={"tm": up}, device_id_type=MESH_ID,
        ),
        pltpu.make_async_remote_copy(
            src_ref=record_hbm.at[pl.ds(0, RIM)], dst_ref=above,
            send_sem=halo_send.at[1], recv_sem=halo_recv.at[1],
            device_id={"tm": down}, device_id_type=MESH_ID,
        ),
    ]
    for halo in halos:
        halo.start()

    def block_copy(source, target, send_sem, recv_sem, peer):
        return pltpu.make_async_remote_copy(
            src_ref=source, dst_ref=target, send_sem=send_sem, recv_sem=recv_sem,
            device_id={"chan": peer}, device_id_type=MESH_ID,
        )

    relay = 2 * ((zed + RING - 4) % RING) + side
    origin = 2 * ((zed + 4) % RING) + side

    def exchange(source, target, hold, chunk, way, send_sem, recv_sem):
        far = peer_of(FAR, zed, side)
        block_copy(
            source.at[chunk, far], hold.at[chunk], send_sem.at[chunk],
            hold_recv.at[way, chunk], relay,
        ).start()

        for first, last in ((1, FAR), (FAR + 1, GROUPS)):
            @pl.loop(first, last)
            def _(step):
                peer = peer_of(step, zed, side)
                block_copy(
                    source.at[chunk, peer], target.at[chunk, me], send_sem.at[chunk],
                    recv_sem.at[chunk], peer,
                ).start()

        target[chunk, me] = source[chunk, me]

    def forward(target, hold, chunk, way, recv_sem):
        copy = block_copy(
            hold.at[chunk], target.at[chunk, origin], hold_send.at[way, chunk],
            recv_sem.at[chunk], peer_of(FAR, origin // 2, side),
        )
        pltpu.make_async_copy(hold.at[chunk], hold.at[chunk], hold_recv.at[way, chunk]).wait()
        copy.start()
        forwards.append(copy)

    forwards = []

    def all_of(buffer, chunk, sem):
        span = buffer.at[chunk, pl.ds(0, GROUPS - 1)]
        return pltpu.make_async_copy(span, span, sem.at[chunk])

    for load in loads[:2]:
        load.wait()
    for halo in halos:
        halo.wait_recv()

    keep_low = jnp.where(tm > 0, 1.0, 0.0).astype(jnp.float32)
    keep_high = jnp.where(tm < count - 1, 1.0, 0.0).astype(jnp.float32)

    @pl.loop(0, RIM // 64)
    def _(i):
        rows = pl.ds(pl.multiple_of(i * 64, 64), 64)
        upper = pl.ds(pl.multiple_of(RIM + i * 64, 64), 64)
        a = below[rows] * (taper[rows] * keep_low)
        b = record[upper] * taper[pl.ds(pl.multiple_of(HOP + i * 64, 64), 64)]
        c = record[rows] * taper[upper]
        d = above[rows] * (taper[pl.ds(pl.multiple_of(HOP + RIM + i * 64, 64), 64)] * keep_high)
        for where, first, second in ((rows, a, b), (upper, c, d)):
            high, low = halves(first + second)
            rhs[0, where, 0:LANES] = high
            rhs[0, where, LANES : 2 * LANES] = low
            high, low = halves(first - second)
            rhs[1, where, 0:LANES] = high
            rhs[1, where, LANES : 2 * LANES] = low

    def time_rows(parity, rows, first=0, span=HOP):
        cols = slice(first, first + span)
        wide = dot(time[2 * parity, rows, cols], rhs[parity, cols])
        tail = dot(time[2 * parity + 1, rows, cols], rhs[parity, cols, 0:LANES])
        return wide[:, 0:LANES] + wide[:, LANES : 2 * LANES] + tail

    for chunk in range(CHUNKS):
        parity, s = chunk // SUB, chunk % SUB
        if s == 0:
            loads[2 + 2 * parity].wait()
            loads[3 + 2 * parity].wait()

        @pl.loop(0, SPAN // BLOCK)
        def _(i):
            rows = pl.ds(pl.multiple_of(s * SPAN + i * BLOCK, BLOCK), BLOCK)
            cells = time_rows(parity, rows).reshape(BLOCK // ROWS, ROWS, LANES)
            send[chunk, pl.ds(i * (BLOCK // ROWS), BLOCK // ROWS)] = cells

        if chunk > 0:
            forward(recv, go_hold, chunk - 1, 0, go_recv)
        exchange(send, recv, go_hold, chunk, 0, go_send, go_recv)

    forward(recv, go_hold, CHUNKS - 1, 0, go_recv)
    for load in loads[6:]:
        load.wait()

    for chunk in range(CHUNKS):
        parity, s = chunk // SUB, chunk % SUB
        row = lax.broadcasted_iota(jnp.int32, (ROWS, 1), 0)
        freq = 2 * (SPAN * s + ROWS * me + row) + parity
        band = jnp.minimum(jnp.minimum(freq, WIN - freq), HOP - 1)
        limit = jnp.zeros((ROWS, LANES), jnp.int32)
        for i in range(HOP // LANES):
            here = i * LANES + lax.broadcasted_iota(jnp.int32, (ROWS, LANES), 1)
            limit = limit + jnp.where(here == band, cuts[0:1, i * LANES : (i + 1) * LANES], 0)
        limit = jnp.sum(limit, axis=1, keepdims=True)

        all_of(recv, chunk, go_recv).wait()

        @pl.loop(0, ROWS // 8)
        def _(i):
            rows = pl.ds(pl.multiple_of(i * 8, 8), 8)
            lines = real_dft([recv[chunk, d, rows] for d in range(GROUPS)])
            for p, (re, im) in enumerate(lines):
                if p == 0:
                    spec[p, rows, 0:LANES] = re
                    spec[p, rows, LANES : 2 * LANES] = jnp.zeros_like(re)
                elif im is None:
                    spec[p, rows, 0:LANES] = re * twist[0, p]
                    spec[p, rows, LANES : 2 * LANES] = -(re * twist[1, p])
                else:
                    c, sn = twist[0, p], twist[1, p]
                    spec[p, rows, 0:LANES] = re * c + im * sn
                    spec[p, rows, LANES : 2 * LANES] = im * c - re * sn

        lines = spec[...].reshape(PARTS * ROWS, 2 * LANES)
        values = table_product(lines, chan[0], chan[1]).reshape(PARTS, ROWS, 2 * LANES)
        kept = jnp.where(wave[:, 0:1] <= limit[None], values, 0.0)
        lines = kept.reshape(PARTS * ROWS, 2 * LANES)
        spec[...] = table_product(lines, chan[2], chan[3]).reshape(PARTS, ROWS, 2 * LANES)

        @pl.loop(0, ROWS // 8)
        def _(i):
            rows = pl.ds(pl.multiple_of(i * 8, 8), 8)
            lines = []
            for p in range(PARTS):
                re, im = spec[p, rows, 0:LANES], spec[p, rows, LANES : 2 * LANES]
                c, sn = twist[0, p], twist[1, p]
                if p == 0:
                    lines.append((re, None))
                elif p == PARTS - 1:
                    lines.append((re * c - im * sn, None))
                else:
                    lines.append((re * c - im * sn, im * c + re * sn))
            for d, value in enumerate(real_inverse(lines)):
                turned[chunk, d, rows] = value

        exchange(turned, back, ret_hold, chunk, 1, ret_send, ret_recv)
        forward(back, ret_hold, chunk, 1, ret_recv)

    scale = 1.0 / (WIN * NCH)
    totals = (part, part_odd)
    for chunk in range(CHUNKS):
        parity, s = chunk // SUB, chunk % SUB
        all_of(back, chunk, ret_recv).wait()

        @pl.loop(0, SPAN // BLOCK)
        def _(i):
            where = pl.ds(pl.multiple_of(s * SPAN + i * BLOCK, BLOCK), BLOCK)
            blocks = back[chunk, pl.ds(i * (BLOCK // ROWS), BLOCK // ROWS)]
            high, low = halves(blocks.reshape(BLOCK, LANES))
            rhs[parity, where, 0:LANES] = high
            rhs[parity, where, LANES : 2 * LANES] = low

        if chunk == CHUNKS - 1:
            break

        @pl.loop(0, HOP // BLOCK)
        def _(i):
            rows = pl.ds(pl.multiple_of(i * BLOCK, BLOCK), BLOCK)
            value = time_rows(parity, rows, s * SPAN, SPAN)
            totals[parity][rows] = value if s == 0 else totals[parity][rows] + value

    spills = []
    for i in range(HOP // BLOCK):
        here = slice(i * BLOCK, (i + 1) * BLOCK)
        odd = time_rows(1, here, (SUB - 1) * SPAN, SPAN)
        if SUB > 1:
            odd = odd + part_odd[here]
        even = part[here]
        first = (even + odd) * (taper[here] * scale)
        second = (even - odd) * (taper[HOP + i * BLOCK : HOP + (i + 1) * BLOCK] * scale)
        if i < RIM // BLOCK:
            rows = slice(i * BLOCK, (i + 1) * BLOCK)
            pair[0, rows] = first
            out[RIM + i * BLOCK : RIM + (i + 1) * BLOCK] = second
            source, target, other = pair.at[0, rows], low_in.at[rows], down
        else:
            rows = slice(i * BLOCK - RIM, (i + 1) * BLOCK - RIM)
            out[rows] = first
            pair[1, rows] = second
            source, target, other = pair.at[1, rows], high_in.at[rows], up
        spills.append(
            pltpu.make_async_remote_copy(
                src_ref=source, dst_ref=target,
                send_sem=spill_send.at[i], recv_sem=spill_recv.at[i],
                device_id={"tm": other}, device_id_type=MESH_ID,
            )
        )
        spills[-1].start()

    for i, spill in enumerate(spills):
        spill.wait_recv()
        if i < RIM // BLOCK:
            rows, base, extra, keep = slice(i * BLOCK, (i + 1) * BLOCK), RIM, low_in, keep_high
        else:
            rows, base, extra, keep = slice(i * BLOCK - RIM, (i + 1) * BLOCK - RIM), 0, high_in, keep_low
        here = slice(base + rows.start, base + rows.stop)
        out[here] = out[here] + extra[rows] * keep

    for chunk in range(CHUNKS):
        all_of(send, chunk, go_send).wait()
        all_of(turned, chunk, ret_send).wait()
    for copy in halos + spills + forwards:
        copy.wait_send()


def per_device(record, cuts):
    time, taper, chan, twist, wave = tables()
    vmem = pl.BlockSpec(memory_space=pltpu.VMEM)
    hbm = pl.BlockSpec(memory_space=pltpu.HBM)
    blocks = (CHUNKS, GROUPS, ROWS, LANES)
    dma = pltpu.SemaphoreType.DMA
    return pl.pallas_call(
        body,
        out_shape=jax.ShapeDtypeStruct(record.shape, jnp.float32),
        in_specs=[hbm] * 7,
        out_specs=vmem,
        scratch_shapes=[
            pltpu.VMEM(record.shape, jnp.float32),
            pltpu.VMEM(cuts.shape, jnp.int32),
            pltpu.VMEM(time.shape, jnp.bfloat16),
            pltpu.VMEM(taper.shape, jnp.float32),
            pltpu.VMEM(chan.shape, jnp.bfloat16),
            pltpu.VMEM(twist.shape, jnp.float32),
            pltpu.VMEM(wave.shape, jnp.int32),
            pltpu.VMEM((RIM, LANES), jnp.float32),
            pltpu.VMEM((RIM, LANES), jnp.float32),
            pltpu.VMEM((2, RIM, LANES), jnp.float32),
            pltpu.VMEM((2, HOP, 2 * LANES), jnp.bfloat16),
            pltpu.VMEM(blocks, jnp.float32),
            pltpu.VMEM(blocks, jnp.float32),
            pltpu.VMEM((PARTS, ROWS, 2 * LANES), jnp.float32),
            pltpu.VMEM(blocks, jnp.float32),
            pltpu.VMEM(blocks, jnp.float32),
            pltpu.VMEM((HOP, LANES), jnp.float32),
            pltpu.VMEM((HOP, LANES), jnp.float32),
            pltpu.VMEM((RIM, LANES), jnp.float32),
            pltpu.VMEM((RIM, LANES), jnp.float32),
            pltpu.VMEM((CHUNKS, ROWS, LANES), jnp.float32),
            pltpu.VMEM((CHUNKS, ROWS, LANES), jnp.float32),
            dma((10,)), dma((2,)), dma((2,)), dma((4,)), dma((4,)),
            dma((CHUNKS,)), dma((CHUNKS,)), dma((CHUNKS,)), dma((CHUNKS,)),
            dma((2, CHUNKS)), dma((2, CHUNKS)),
        ],
        compiler_params=pltpu.CompilerParams(
            collective_id=0, has_side_effects=True, vmem_limit_bytes=60 * 1024 * 1024
        ),
    )(record, cuts, time, taper, chan, twist, wave)


def solution(mesh):
    return jax.shard_map(
        per_device,
        mesh=mesh,
        in_specs=(P("tm", "chan"), P("tm", None)),
        out_specs=P("tm", "chan"),
        check_vma=False,
    )
```

profile of v0, /device:TPU:16, one launch (start us, length us, event | category | flops | bytes accessed | tf_op | source)
XLA Modules:
  0.0 135.4 jit_solution(12265551426499385680)
XLA Ops:
  0.0 133.5 %shard_map.73 = f32[1024,128]{1,0:T(8,128)} custom-call(f32[1024,128]{1,0:T(8,128)} %record_hbm.1, s32[1,1024]{1,0:T(1,128)} %cuts_hbm.1, bf16[4,1024,1024]{2,1,0:T(8,128)(2,1)} %constant.10.clone.time_hbm, f32[2048,128]{1,0:T(8,128)} %constant.11.clone.taper_hbm, bf16[4,256,256]{2,1,0:T(8,128)(2,1)} %constant.12.clone.chan_hbm, ...), custom_call_target="tpu_custom_call" | custom-call | tf_op jit(solution)/shard_map/pallas_call | solution.py:416
  133.5 1.9 %copy.9 = f32[1024,128]{1,0:T(8,128)} copy(f32[1024,128]{1,0:T(8,128)} %shard_map.73) | data formatting | bytes 1048576
where the time goes:
time: 136 us; the launch traced here: 135 us
  Pallas kernels  133 us (98%)
  local copies, waits for them, and re-layouts  1.87 us (1%)
    pallas_call x1, Pallas kernels, per_device(): pl.pallas_call(body, out_shape=jax.ShapeDtypeStruct(record.shape, jnp.flo...  133 us

commit v1 on v0

v1 whole, which is shorter than its diff:
```python
import functools
import math

import jax
import jax.numpy as jnp
import ml_dtypes
import numpy as np
from jax import lax
from jax.experimental import pallas as pl
from jax.experimental.pallas import tpu as pltpu
from jax.sharding import PartitionSpec as P

WIN = 2048
HOP = WIN // 2
RIM = HOP // 2
NCH = 4096
GROUPS = 32
LANES = 128
RING = 16
PARTS = 17
CHUNKS = 2
ROWS = 16
HALF = GROUPS // 2
BLOCK = 256
MESH_ID = pl.DeviceIdType.MESH


def split_bf16(table):
    high = table.astype(np.float32).astype(ml_dtypes.bfloat16)
    low = (table - high.astype(np.float64)).astype(ml_dtypes.bfloat16)
    return np.stack([high, low])


def cas(angle):
    return np.cos(angle) + np.sin(angle)


@functools.cache
def tables():
    index = np.arange(HOP)
    even = cas(2.0 * np.pi / HOP * (np.outer(index, index) % HOP))
    odd_index = 2 * index + 1
    odd = cas(2.0 * np.pi / (2 * WIN) * (np.outer(odd_index, odd_index) % (2 * WIN)))
    time = np.concatenate([split_bf16(even), split_bf16(odd)])
    taper = np.sin(np.pi / WIN * np.arange(WIN)) ** 2
    taper = np.repeat(taper[:, None], LANES, axis=1).astype(np.float32)
    lane = np.arange(LANES)
    angle = 2.0 * np.pi / LANES * (np.outer(lane, lane) % LANES)
    cosine, sine = np.cos(angle), np.sin(angle)
    forward = np.block([[cosine, -sine], [sine, cosine]])
    inverse = np.block([[cosine, sine], [-sine, cosine]])
    chan = np.concatenate([split_bf16(forward), split_bf16(inverse)])
    angle = 2.0 * np.pi / NCH * np.outer(np.arange(PARTS), lane)
    twist = np.stack([np.cos(angle), np.sin(angle)]).astype(np.float32)
    twist = np.repeat(twist[:, :, None, :], 8, axis=2)
    return time, taper, chan, twist


def real_dft(x):
    n = len(x)
    if n == 1:
        return [(x[0], None)]
    if n == 2:
        return [(x[0] + x[1], None), (x[0] - x[1], None)]
    even = real_dft(x[0::2])
    odd = real_dft(x[1::2])
    half = n // 2
    out = [None] * (half + 1)
    out[0] = (even[0][0] + odd[0][0], None)
    out[half] = (even[0][0] - odd[0][0], None)
    for k in range(1, half // 2 + 1):
        e_re, e_im = even[k]
        o_re, o_im = odd[k]
        if 2 * k == half:
            out[k] = (e_re, -o_re)
            continue
        c, s = math.cos(2.0 * math.pi * k / n), math.sin(2.0 * math.pi * k / n)
        t_re = c * o_re + s * o_im
        t_im = c * o_im - s * o_re
        out[k] = (e_re + t_re, e_im + t_im)
        out[half - k] = (e_re - t_re, t_im - e_im)
    return out


def real_inverse(spec):
    half = len(spec) - 1
    n = 2 * half
    first, last = spec[0][0], spec[half][0]
    if n == 2:
        return [first + last, first - last]
    even = [None] * (half // 2 + 1)
    odd = [None] * (half // 2 + 1)
    even[0] = (first + last, None)
    odd[0] = (first - last, None)
    for k in range(1, half // 2 + 1):
        a_re, a_im = spec[k]
        if 2 * k == half:
            even[k] = (2.0 * a_re, None)
            odd[k] = (-2.0 * a_im, None)
            continue
        b_re, b_im = spec[half - k]
        even[k] = (a_re + b_re, a_im - b_im)
        d_re, d_im = a_re - b_re, a_im + b_im
        c, s = math.cos(2.0 * math.pi * k / n), math.sin(2.0 * math.pi * k / n)
        odd[k] = (c * d_re - s * d_im, c * d_im + s * d_re)
    y_even = real_inverse(even)
    y_odd = real_inverse(odd)
    out = []
    for a, b in zip(y_even, y_odd):
        out += [a, b]
    return out


def dot(a, b):
    return jnp.dot(a, b, preferred_element_type=jnp.float32)


def halves(x):
    high = x.astype(jnp.bfloat16)
    low = (x - high.astype(jnp.float32)).astype(jnp.bfloat16)
    return high, low


def table_product(x, high_table, low_table):
    high, low = halves(x)
    return dot(high, high_table) + dot(high, low_table) + dot(low, high_table)


def body(
    record_hbm, cuts_hbm, time_hbm, taper_hbm, chan_hbm, twist_hbm,
    out,
    cuts, time, taper, chan, twist,
    stage, recv, spec, coef, block, below, above, limit, rhs, back_rhs, part,
    own, spill_low, spill_high, low_in, high_in, arrived, turned, stage_back,
    load_sem, cut_send, cut_sem,
    rows_send, rows_recv, ring_send, ring_recv, wave_send, wave_recv, halo_send, halo_recv,
    spill_send, spill_recv, lines_send, lines_recv, home_send, home_recv, last_send, last_recv,
):
    tm = lax.axis_index("tm")
    chan_index = lax.axis_index("chan")
    zed, side = chan_index // 2, chan_index % 2
    place = 2 * tm + side

    def in_plane(other):
        return {"tm": other // 2, "chan": 2 * zed + other % 2}

    def in_ring(other):
        return {"chan": 2 * other + side}

    up = (zed + 1) % RING
    down = (zed + RING - 1) % RING

    loads = [pltpu.make_async_copy(taper_hbm, taper, load_sem.at[0])]
    for i in range(4):
        loads.append(pltpu.make_async_copy(time_hbm.at[i], time.at[i], load_sem.at[1 + i]))
    loads += [
        pltpu.make_async_copy(chan_hbm, chan, load_sem.at[5]),
        pltpu.make_async_copy(twist_hbm, twist, load_sem.at[6]),
    ]

    def piece(other, chunk):
        return record_hbm.at[pl.ds(pl.multiple_of(32 * other + ROWS * chunk, ROWS), ROWS)]

    mine = [
        pltpu.make_async_copy(piece(place, c), stage.at[c, place], load_sem.at[7 + c])
        for c in range(CHUNKS)
    ]

    barrier = pltpu.get_barrier_semaphore()

    @pl.loop(1, GROUPS)
    def _(step):
        other = (place + 11 * step) % GROUPS
        pl.semaphore_signal(barrier, inc=1, device_id=in_plane(other), device_id_type=MESH_ID)

    @pl.loop(1, RING)
    def _(step):
        other = (zed + 7 * step) % RING
        pl.semaphore_signal(barrier, inc=1, device_id=in_ring(other), device_id_type=MESH_ID)

    for load in mine + loads:
        load.start()

    pl.semaphore_wait(barrier, GROUPS + RING - 2)

    def remote(source, target, send_sem, recv_sem, device):
        return pltpu.make_async_remote_copy(
            src_ref=source, dst_ref=target, send_sem=send_sem, recv_sem=recv_sem,
            device_id=device, device_id_type=MESH_ID,
        )

    def plane_exchange(source_of, target, send_sem, recv_sem):
        @pl.loop(1, GROUPS)
        def _(step):
            other = (place + 11 * step) % GROUPS
            remote(source_of(other), target, send_sem, recv_sem, in_plane(other)).start()

    def ring_exchange(source, target, chunk, send_sem, recv_sem):
        @pl.loop(1, RING)
        def _(step):
            other = (zed + 7 * step) % RING
            remote(
                source.at[chunk, pl.ds(2 * other, 2)], target.at[chunk, pl.ds(2 * zed, 2)],
                send_sem.at[chunk], recv_sem.at[chunk], in_ring(other),
            ).start()

        for i in range(2):
            target[chunk, 2 * zed + i] = source[chunk, 2 * zed + i]

    def bytes_of(buffer, count, sem):
        span = buffer.at[0, pl.ds(0, count)]
        return pltpu.make_async_copy(span, span, sem)

    def plane_wait(sem):
        bytes_of(recv, GROUPS - 1, sem).wait()

    def ring_wait(sem):
        bytes_of(recv, GROUPS - 2, sem).wait()

    for c in range(CHUNKS):
        plane_exchange(
            lambda other: piece(other, c), stage.at[c, place], rows_send.at[c], rows_recv.at[c]
        )

    @pl.when(tm == zed)
    def _():
        @pl.loop(1, RING)
        def _(step):
            other = (tm + step) % RING
            remote(cuts_hbm, cuts, cut_send.at[step], cut_sem.at[0], {"tm": other}).start()

        copy = pltpu.make_async_copy(cuts_hbm, cuts, cut_sem.at[1])
        copy.start()
        copy.wait()

    for c in range(CHUNKS):
        mine[c].wait()
        plane_wait(rows_recv.at[c])
        ring_exchange(stage, recv, c, ring_send, ring_recv)

    @pl.when(tm != zed)
    def _():
        remote(cuts_hbm, cuts, cut_send.at[0], cut_sem.at[0], {"tm": zed}).wait_recv()

    for parity in range(2):
        @pl.loop(0, HOP // 32)
        def _(j):
            row = lax.broadcasted_iota(jnp.int32, (32, 1), 0)
            freq = 2 * (32 * j + row) + parity
            band = jnp.minimum(jnp.minimum(freq, WIN - freq), HOP - 1)
            total = jnp.zeros((32, LANES), jnp.int32)
            for i in range(HOP // LANES):
                here = i * LANES + lax.broadcasted_iota(jnp.int32, (32, LANES), 1)
                total = total + jnp.where(here == band, cuts[0:1, i * LANES : (i + 1) * LANES], 0)
            total = jnp.sum(total, axis=1, keepdims=True)
            rows = pl.ds(pl.multiple_of(j * 32, 32), 32)
            limit[parity, rows] = jnp.broadcast_to(total, (32, LANES))

    for load in loads:
        load.wait()

    whole = 2 * LANES
    for c in range(CHUNKS):
        ring_wait(ring_recv.at[c])

        @pl.loop(0, ROWS // 8)
        def _(i):
            rows = pl.ds(pl.multiple_of(i * 8, 8), 8)
            lines = real_dft([recv[c, d, rows] for d in range(GROUPS)])
            for p, (re, im) in enumerate(lines):
                if p == 0:
                    spec[p, rows, 0:LANES] = re
                    spec[p, rows, LANES:whole] = jnp.zeros_like(re)
                elif im is None:
                    spec[p, rows, 0:LANES] = re * twist[0, p]
                    spec[p, rows, LANES:whole] = -(re * twist[1, p])
                else:
                    cosine, sine = twist[0, p], twist[1, p]
                    spec[p, rows, 0:LANES] = re * cosine + im * sine
                    spec[p, rows, LANES:whole] = im * cosine - re * sine

        lines = spec[...].reshape(PARTS * ROWS, whole)
        lines = table_product(lines, chan[0], chan[1]).reshape(PARTS, ROWS, whole)
        for p in range(PARTS):
            re, im = lines[p, :, 0:LANES], lines[p, :, LANES:whole]
            if p == 0:
                coef[c, 0] = re - im
            elif p == PARTS - 1:
                coef[c, GROUPS - 1] = re - im
            else:
                coef[c, 2 * p - 1] = re
                coef[c, 2 * p] = im

        plane_exchange(
            lambda other: coef.at[c, other], block.at[c, place], wave_send.at[c], wave_recv.at[c]
        )
        block[c, place] = coef[c, place]

    halos = []
    for c in range(CHUNKS):
        plane_wait(wave_recv.at[c])
        halos += [
            remote(
                block.at[c, pl.ds(HALF, HALF)], below.at[c],
                halo_send.at[2 * c], halo_recv.at[2 * c], in_ring(up),
            ),
            remote(
                block.at[c, pl.ds(0, HALF)], above.at[c],
                halo_send.at[2 * c + 1], halo_recv.at[2 * c + 1], in_ring(down),
            ),
        ]
        for halo in halos[-2:]:
            halo.start()

    keep_low = jnp.where(zed > 0, 1.0, 0.0).astype(jnp.float32)
    keep_high = jnp.where(zed < RING - 1, 1.0, 0.0).astype(jnp.float32)

    for c in range(CHUNKS):
        for halo in halos[2 * c : 2 * c + 2]:
            halo.wait_recv()

        @pl.loop(0, HALF)
        def _(q):
            def at(base):
                return pl.ds(pl.multiple_of(base + 32 * q + ROWS * c, ROWS), ROWS)

            first = below[c, q] * (taper[at(0)] * keep_low)
            second = block[c, HALF + q] * taper[at(HOP)]
            third = block[c, q] * taper[at(RIM)]
            fourth = above[c, q] * (taper[at(HOP + RIM)] * keep_high)
            for where, one, two in ((at(0), first, second), (at(RIM), third, fourth)):
                high, low = halves(one + two)
                rhs[0, where, 0:LANES] = high
                rhs[0, where, LANES:whole] = low
                high, low = halves(one - two)
                rhs[1, where, 0:LANES] = high
                rhs[1, where, LANES:whole] = low

    def time_rows(source, parity, rows):
        wide = dot(time[2 * parity, rows], source[parity])
        tail = dot(time[2 * parity + 1, rows], source[parity, :, 0:LANES])
        return wide[:, 0:LANES] + wide[:, LANES:whole] + tail

    lane = lax.broadcasted_iota(jnp.int32, (1, LANES), 1)
    wave = (place + 1) // 2 + GROUPS * lane
    wave = jnp.minimum(wave, NCH - wave)

    for parity in range(2):
        @pl.loop(0, HOP // BLOCK)
        def _(i):
            rows = pl.ds(pl.multiple_of(i * BLOCK, BLOCK), BLOCK)
            values = time_rows(rhs, parity, rows)
            high, low = halves(jnp.where(wave <= limit[parity, rows], values, 0.0))
            back_rhs[parity, rows, 0:LANES] = high
            back_rhs[parity, rows, LANES:whole] = low

    @pl.loop(0, HOP // BLOCK)
    def _(i):
        rows = pl.ds(pl.multiple_of(i * BLOCK, BLOCK), BLOCK)
        part[rows] = time_rows(back_rhs, 0, rows)

    scale = 1.0 / (WIN * NCH)
    pieces = BLOCK // ROWS
    spills = []
    for i in (2, 3, 0, 1):
        here = slice(i * BLOCK, (i + 1) * BLOCK)
        even = part[here]
        odd = time_rows(back_rhs, 1, here)
        first = (even + odd) * (taper[here] * scale)
        second = (even - odd) * (taper[HOP + i * BLOCK : HOP + (i + 1) * BLOCK] * scale)
        first = first.reshape(pieces, ROWS, LANES)
        second = second.reshape(pieces, ROWS, LANES)
        at = pl.ds(i % 2 * pieces, pieces)
        if i < 2:
            own[1, at] = second
            spill_low[at] = first
            source, target, other = spill_low.at[at], low_in.at[at], down
        else:
            own[0, at] = first
            spill_high[at] = second
            source, target, other = spill_high.at[at], high_in.at[at], up
        spills.append(remote(source, target, spill_send.at[i], spill_recv.at[i], in_ring(other)))
        spills[-1].start()

    for c in range(CHUNKS):
        for spill in spills[2 * c : 2 * c + 2]:
            spill.wait_recv()
        extra, keep = ((high_in, keep_low), (low_in, keep_high))[c]

        @pl.loop(0, GROUPS)
        def _(q):
            own[c, q] = own[c, q] + extra[q] * keep

        plane_exchange(
            lambda other: own.at[c, other], arrived.at[c, place], lines_send.at[c], lines_recv.at[c]
        )
        arrived[c, place] = own[c, place]

    for c in range(CHUNKS):
        plane_wait(lines_recv.at[c])
        for p in range(PARTS):
            if p == 0 or p == PARTS - 1:
                re = arrived[c, 0 if p == 0 else GROUPS - 1]
                im = -re
            else:
                re, im = arrived[c, 2 * p - 1], arrived[c, 2 * p]
            spec[p, :, 0:LANES] = re
            spec[p, :, LANES:whole] = im
        lines = spec[...].reshape(PARTS * ROWS, whole)
        spec[...] = table_product(lines, chan[2], chan[3]).reshape(PARTS, ROWS, whole)

        @pl.loop(0, ROWS // 8)
        def _(i):
            rows = pl.ds(pl.multiple_of(i * 8, 8), 8)
            lines = []
            for p in range(PARTS):
                re, im = spec[p, rows, 0:LANES], spec[p, rows, LANES:whole]
                cosine, sine = twist[0, p], twist[1, p]
                if p == 0:
                    lines.append((re, None))
                elif p == PARTS - 1:
                    lines.append((re * cosine - im * sine, None))
                else:
                    lines.append((re * cosine - im * sine, im * cosine + re * sine))
            for d, value in enumerate(real_inverse(lines)):
                turned[c, d, rows] = value

        ring_exchange(turned, stage_back, c, home_send, home_recv)

    def final(c):
        return pl.ds(pl.multiple_of(RIM * c + ROWS * place, ROWS), ROWS)

    for c in range(CHUNKS):
        ring_wait(home_recv.at[c])
        plane_exchange(
            lambda other: stage_back.at[c, other], out.at[final(c)], last_send.at[c], last_recv.at[c]
        )
        out[final(c)] = stage_back[c, place]

    for c in range(CHUNKS):
        plane_wait(last_recv.at[c])
    for c in range(CHUNKS):
        for sem in (rows_send, wave_send, lines_send, last_send):
            plane_wait(sem.at[c])
        for sem in (ring_send, home_send):
            ring_wait(sem.at[c])
    for copy in halos + spills:
        copy.wait_send()

    @pl.when(tm == zed)
    def _():
        @pl.loop(1, RING)
        def _(step):
            other = (tm + step) % RING
            remote(cuts_hbm, cuts, cut_send.at[step], cut_sem.at[0], {"tm": other}).wait_send()


def per_device(record, cuts):
    time, taper, chan, twist = tables()
    blocks = pltpu.VMEM((CHUNKS, GROUPS, ROWS, LANES), jnp.float32)
    half = pltpu.VMEM((CHUNKS, HALF, ROWS, LANES), jnp.float32)
    rim = pltpu.VMEM((GROUPS, ROWS, LANES), jnp.float32)
    sides = pltpu.VMEM((2, HOP, 2 * LANES), jnp.bfloat16)
    dma = pltpu.SemaphoreType.DMA
    return pl.pallas_call(
        body,
        out_shape=jax.ShapeDtypeStruct(record.shape, jnp.float32),
        in_specs=[pl.BlockSpec(memory_space=pltpu.HBM)] * 6,
        out_specs=pl.BlockSpec(memory_space=pltpu.VMEM),
        scratch_shapes=[
            pltpu.VMEM(cuts.shape, jnp.int32),
            pltpu.VMEM(time.shape, jnp.bfloat16),
            pltpu.VMEM(taper.shape, jnp.float32),
            pltpu.VMEM(chan.shape, jnp.bfloat16),
            pltpu.VMEM(twist.shape, jnp.float32),
            blocks, blocks,
            pltpu.VMEM((PARTS, ROWS, 2 * LANES), jnp.float32),
            blocks, blocks, half, half,
            pltpu.VMEM((2, HOP, LANES), jnp.int32),
            sides, sides,
            pltpu.VMEM((HOP, LANES), jnp.float32),
            blocks, rim, rim, rim, rim, blocks, blocks, blocks,
            dma((9,)), dma((RING,)), dma((2,)),
            dma((2,)), dma((2,)), dma((2,)), dma((2,)), dma((2,)), dma((2,)), dma((4,)), dma((4,)),
            dma((4,)), dma((4,)), dma((2,)), dma((2,)), dma((2,)), dma((2,)), dma((2,)), dma((2,)),
        ],
        compiler_params=pltpu.CompilerParams(
            collective_id=0, has_side_effects=True, vmem_limit_bytes=60 * 1024 * 1024
        ),
    )(record, cuts, time, taper, chan, twist)


def solution(mesh):
    return jax.shard_map(
        per_device,
        mesh=mesh,
        in_specs=(P("tm", "chan"), P("tm", None)),
        out_specs=P("tm", "chan"),
        check_vma=False,
    )
```

time: 136 us -> 120 us (0.88)
  the two profiles are of different devices: /device:TPU:16 before, /device:TPU:1 now
where the time goes in v1:
time: 120 us; the launch traced here: 119 us
  Pallas kernels  117 us (98%)
  local copies, waits for them, and re-layouts  1.87 us (2%)
    pallas_call x1, Pallas kernels, per_device(): pl.pallas_call(body, out_shape=jax.ShapeDtypeStruct(record.shape, jnp.flo...  117 us

profile of v1, /device:TPU:1, one launch (start us, length us, event | category | flops | bytes accessed | tf_op | source)
XLA Modules:
  0.0 119.0 jit_solution(2228584408424205361)
XLA Ops:
  0.0 117.1 %shard_map.64 = f32[1024,128]{1,0:T(8,128)} custom-call(f32[1024,128]{1,0:T(8,128)} %record_hbm.1, s32[1,1024]{1,0:T(1,128)} %cuts_hbm.1, bf16[4,1024,1024]{2,1,0:T(8,128)(2,1)} %constant.8.clone.time_hbm, f32[2048,128]{1,0:T(8,128)} %constant.9.clone.taper_hbm, bf16[4,256,256]{2,1,0:T(8,128)(2,1)} %constant.10.clone.chan_hbm, ...), custom_call_target="tpu_custom_call" | custom-call | tf_op jit(solution)/shard_map/pallas_call | solution.py:465
  117.1 1.9 %copy.8 = f32[1024,128]{1,0:T(8,128)} copy(f32[1024,128]{1,0:T(8,128)} %shard_map.64) | data formatting | bytes 1048576

commit v2 on v1

--- a/solution.py
+++ b/solution.py
@@ -18,10 +18,12 @@
 LANES = 128
 RING = 16
 PARTS = 17
-CHUNKS = 2
-ROWS = 16
+CHUNKS = 4
+ROWS = 32 // CHUNKS
 HALF = GROUPS // 2
-BLOCK = 256
+TALL = WIN // LANES
+TIMES = TALL // 2
+PER_CHUNK = 8 // CHUNKS
 MESH_ID = pl.DeviceIdType.MESH
 
 
@@ -37,11 +39,20 @@
 
 @functools.cache
 def tables():
-    index = np.arange(HOP)
-    even = cas(2.0 * np.pi / HOP * (np.outer(index, index) % HOP))
-    odd_index = 2 * index + 1
-    odd = cas(2.0 * np.pi / (2 * WIN) * (np.outer(odd_index, odd_index) % (2 * WIN)))
-    time = np.concatenate([split_bf16(even), split_bf16(odd)])
+    point = np.arange(LANES)
+    blocks = []
+    for p in range(TIMES):
+        freq = p + TALL * point
+        angle = 2.0 * np.pi / WIN * (np.outer(freq, point) % WIN)
+        cosine, sine = np.cos(angle), np.sin(angle)
+        if p == 0:
+            middle = 2.0 * np.pi / WIN * (np.outer(TIMES + freq, point) % WIN)
+            none = np.zeros_like(angle)
+            blocks.append(np.block([[cas(angle), none], [none, cas(middle)]]))
+        else:
+            blocks.append(np.block([[cosine, sine], [-sine, cosine]]))
+    blocks = np.stack(blocks)
+    time = np.stack([split_bf16(blocks), split_bf16(blocks.transpose(0, 2, 1))])
     taper = np.sin(np.pi / WIN * np.arange(WIN)) ** 2
     taper = np.repeat(taper[:, None], LANES, axis=1).astype(np.float32)
     lane = np.arange(LANES)
@@ -126,11 +137,19 @@
     return dot(high, high_table) + dot(high, low_table) + dot(low, high_table)
 
 
+def div(a, b):
+    return lax.div(a, jnp.int32(b))
+
+
+def rem(a, b):
+    return lax.rem(a, jnp.int32(b))
+
+
 def body(
     record_hbm, cuts_hbm, time_hbm, taper_hbm, chan_hbm, twist_hbm,
     out,
     cuts, time, taper, chan, twist,
-    stage, recv, spec, coef, block, below, above, limit, rhs, back_rhs, part,
+    stage, recv, spec, coef, block, below, above, limit, lines_time,
     own, spill_low, spill_high, low_in, high_in, arrived, turned, stage_back,
     load_sem, cut_send, cut_sem,
     rows_send, rows_recv, ring_send, ring_recv, wave_send, wave_recv, halo_send, halo_recv,
@@ -138,31 +157,30 @@
 ):
     tm = lax.axis_index("tm")
     chan_index = lax.axis_index("chan")
-    zed, side = chan_index // 2, chan_index % 2
+    zed, side = div(chan_index, 2), rem(chan_index, 2)
     place = 2 * tm + side
 
     def in_plane(other):
-        return {"tm": other // 2, "chan": 2 * zed + other % 2}
+        return {"tm": div(other, 2), "chan": 2 * zed + rem(other, 2)}
 
     def in_ring(other):
         return {"chan": 2 * other + side}
 
-    up = (zed + 1) % RING
-    down = (zed + RING - 1) % RING
+    up = rem(zed + 1, RING)
+    down = rem(zed + RING - 1, RING)
 
     loads = [pltpu.make_async_copy(taper_hbm, taper, load_sem.at[0])]
-    for i in range(4):
-        loads.append(pltpu.make_async_copy(time_hbm.at[i], time.at[i], load_sem.at[1 + i]))
     loads += [
-        pltpu.make_async_copy(chan_hbm, chan, load_sem.at[5]),
-        pltpu.make_async_copy(twist_hbm, twist, load_sem.at[6]),
+        pltpu.make_async_copy(chan_hbm, chan, load_sem.at[1]),
+        pltpu.make_async_copy(twist_hbm, twist, load_sem.at[2]),
+        pltpu.make_async_copy(time_hbm, time, load_sem.at[3]),
     ]
 
     def piece(other, chunk):
         return record_hbm.at[pl.ds(pl.multiple_of(32 * other + ROWS * chunk, ROWS), ROWS)]
 
     mine = [
-        pltpu.make_async_copy(piece(place, c), stage.at[c, place], load_sem.at[7 + c])
+        pltpu.make_async_copy(piece(place, c), stage.at[c, place], load_sem.at[4 + c])
         for c in range(CHUNKS)
     ]
 
@@ -170,12 +188,12 @@
 
     @pl.loop(1, GROUPS)
     def _(step):
-        other = (place + 11 * step) % GROUPS
+        other = rem(place + 11 * step, GROUPS)
         pl.semaphore_signal(barrier, inc=1, device_id=in_plane(other), device_id_type=MESH_ID)
 
     @pl.loop(1, RING)
     def _(step):
-        other = (zed + 7 * step) % RING
+        other = rem(zed + 7 * step, RING)
         pl.semaphore_signal(barrier, inc=1, device_id=in_ring(other), device_id_type=MESH_ID)
 
     for load in mine + loads:
@@ -192,13 +210,13 @@
     def plane_exchange(source_of, target, send_sem, recv_sem):
         @pl.loop(1, GROUPS)
         def _(step):
-            other = (place + 11 * step) % GROUPS
+            other = rem(place + 11 * step, GROUPS)
             remote(source_of(other), target, send_sem, recv_sem, in_plane(other)).start()
 
     def ring_exchange(source, target, chunk, send_sem, recv_sem):
         @pl.loop(1, RING)
         def _(step):
-            other = (zed + 7 * step) % RING
+            other = rem(zed + 7 * step, RING)
             remote(
                 source.at[chunk, pl.ds(2 * other, 2)], target.at[chunk, pl.ds(2 * zed, 2)],
                 send_sem.at[chunk], recv_sem.at[chunk], in_ring(other),
@@ -226,7 +244,7 @@
     def _():
         @pl.loop(1, RING)
         def _(step):
-            other = (tm + step) % RING
+            other = rem(tm + step, RING)
             remote(cuts_hbm, cuts, cut_send.at[step], cut_sem.at[0], {"tm": other}).start()
 
         copy = pltpu.make_async_copy(cuts_hbm, cuts, cut_sem.at[1])
@@ -242,11 +260,14 @@
     def _():
         remote(cuts_hbm, cuts, cut_send.at[0], cut_sem.at[0], {"tm": zed}).wait_recv()
 
-    for parity in range(2):
-        @pl.loop(0, HOP // 32)
+    for p in range(TIMES):
+        @pl.loop(0, 8)
         def _(j):
-            row = lax.broadcasted_iota(jnp.int32, (32, 1), 0)
-            freq = 2 * (32 * j + row) + parity
+            row = 32 * j + lax.broadcasted_iota(jnp.int32, (32, 1), 0)
+            if p == 0:
+                freq = jnp.where(row < LANES, TALL * row, TALL * (row - LANES) + TIMES)
+            else:
+                freq = p + TALL * jnp.where(row < LANES, row, row - LANES)
             band = jnp.minimum(jnp.minimum(freq, WIN - freq), HOP - 1)
             total = jnp.zeros((32, LANES), jnp.int32)
             for i in range(HOP // LANES):
@@ -254,7 +275,7 @@
                 total = total + jnp.where(here == band, cuts[0:1, i * LANES : (i + 1) * LANES], 0)
             total = jnp.sum(total, axis=1, keepdims=True)
             rows = pl.ds(pl.multiple_of(j * 32, 32), 32)
-            limit[parity, rows] = jnp.broadcast_to(total, (32, LANES))
+            limit[p, rows] = jnp.broadcast_to(total, (32, LANES))
 
     for load in loads:
         load.wait()
@@ -315,88 +336,93 @@
     keep_low = jnp.where(zed > 0, 1.0, 0.0).astype(jnp.float32)
     keep_high = jnp.where(zed < RING - 1, 1.0, 0.0).astype(jnp.float32)
 
+    quarter = TALL // 4
     for c in range(CHUNKS):
         for halo in halos[2 * c : 2 * c + 2]:
             halo.wait_recv()
 
-        @pl.loop(0, HALF)
-        def _(q):
-            def at(base):
-                return pl.ds(pl.multiple_of(base + 32 * q + ROWS * c, ROWS), ROWS)
-
-            first = below[c, q] * (taper[at(0)] * keep_low)
-            second = block[c, HALF + q] * taper[at(HOP)]
-            third = block[c, q] * taper[at(RIM)]
-            fourth = above[c, q] * (taper[at(HOP + RIM)] * keep_high)
-            for where, one, two in ((at(0), first, second), (at(RIM), third, fourth)):
-                high, low = halves(one + two)
-                rhs[0, where, 0:LANES] = high
-                rhs[0, where, LANES:whole] = low
-                high, low = halves(one - two)
-                rhs[1, where, 0:LANES] = high
-                rhs[1, where, LANES:whole] = low
-
-    def time_rows(source, parity, rows):
-        wide = dot(time[2 * parity, rows], source[parity])
-        tail = dot(time[2 * parity + 1, rows], source[parity, :, 0:LANES])
-        return wide[:, 0:LANES] + wide[:, LANES:whole] + tail
+        @pl.loop(0, 4)
+        def _(a):
+            start = 32 * a + ROWS * c
+            cells = []
+            for i in range(TALL):
+                weight = taper[pl.ds(pl.multiple_of(LANES * i + start, 8), ROWS)]
+                if i < quarter:
+                    cells.append(below[c, 4 * i + a] * (weight * keep_low))
+                elif i < 3 * quarter:
+                    cells.append(block[c, 4 * (i - quarter) + a] * weight)
+                else:
+                    cells.append(above[c, 4 * (i - 3 * quarter) + a] * (weight * keep_high))
+            here = pl.ds(pl.multiple_of(start, 8), ROWS)
+            there = pl.ds(pl.multiple_of(LANES + start, 8), ROWS)
+            for p, (re, im) in enumerate(real_dft(cells)):
+                if p == TIMES:
+                    lines_time[0, there] = re
+                else:
+                    lines_time[p, here] = re
+                    if p > 0:
+                        lines_time[p, there] = im
 
     lane = lax.broadcasted_iota(jnp.int32, (1, LANES), 1)
-    wave = (place + 1) // 2 + GROUPS * lane
+    wave = div(place + 1, 2) + GROUPS * lane
     wave = jnp.minimum(wave, NCH - wave)
 
-    for parity in range(2):
-        @pl.loop(0, HOP // BLOCK)
-        def _(i):
-            rows = pl.ds(pl.multiple_of(i * BLOCK, BLOCK), BLOCK)
-            values = time_rows(rhs, parity, rows)
-            high, low = halves(jnp.where(wave <= limit[parity, rows], values, 0.0))
-            back_rhs[parity, rows, 0:LANES] = high
-            back_rhs[parity, rows, LANES:whole] = low
-
-    @pl.loop(0, HOP // BLOCK)
-    def _(i):
-        rows = pl.ds(pl.multiple_of(i * BLOCK, BLOCK), BLOCK)
-        part[rows] = time_rows(back_rhs, 0, rows)
+    def time_product(way, p, values):
+        high, low = halves(values)
+        wide = dot(time[way, 0, p], jnp.concatenate([high, low], axis=1))
+        return wide[:, 0:LANES] + wide[:, LANES:whole] + dot(time[way, 1, p], high)
+
+    for p in range(TIMES):
+        values = time_product(0, p, lines_time[p])
+        lines_time[p] = time_product(1, p, jnp.where(wave <= limit[p], values, 0.0))
 
     scale = 1.0 / (WIN * NCH)
-    pieces = BLOCK // ROWS
-    spills = []
-    for i in (2, 3, 0, 1):
-        here = slice(i * BLOCK, (i + 1) * BLOCK)
-        even = part[here]
-        odd = time_rows(back_rhs, 1, here)
-        first = (even + odd) * (taper[here] * scale)
-        second = (even - odd) * (taper[HOP + i * BLOCK : HOP + (i + 1) * BLOCK] * scale)
-        first = first.reshape(pieces, ROWS, LANES)
-        second = second.reshape(pieces, ROWS, LANES)
-        at = pl.ds(i % 2 * pieces, pieces)
-        if i < 2:
-            own[1, at] = second
-            spill_low[at] = first
-            source, target, other = spill_low.at[at], low_in.at[at], down
+    per = LANES // ROWS
+
+    @pl.loop(0, per)
+    def _(g):
+        here = pl.ds(pl.multiple_of(ROWS * g, ROWS), ROWS)
+        there = pl.ds(pl.multiple_of(LANES + ROWS * g, ROWS), ROWS)
+        lines = [(lines_time[0, here], None)]
+        for p in range(1, TIMES):
+            lines.append((lines_time[p, here], lines_time[p, there]))
+        lines.append((lines_time[0, there], None))
+        for i, value in enumerate(real_inverse(lines)):
+            weight = taper[pl.ds(pl.multiple_of(LANES * i + ROWS * g, ROWS), ROWS)]
+            value = value * (weight * scale)
+            if i < quarter:
+                target, k = spill_low, i
+            elif i < 3 * quarter:
+                target, k = own, i - quarter
+            else:
+                target, k = spill_high, i - 3 * quarter
+            target[k // PER_CHUNK, per * (k % PER_CHUNK) + g] = value
+
+    spills = {}
+    order = [c for pair in zip(range(CHUNKS // 2), range(CHUNKS // 2, CHUNKS)) for c in pair]
+    for c in order:
+        k = c % (CHUNKS // 2)
+        if c < CHUNKS // 2:
+            source, target, other = spill_high.at[k], high_in.at[k], up
         else:
-            own[0, at] = first
-            spill_high[at] = second
-            source, target, other = spill_high.at[at], high_in.at[at], up
-        spills.append(remote(source, target, spill_send.at[i], spill_recv.at[i], in_ring(other)))
-        spills[-1].start()
-
-    for c in range(CHUNKS):
-        for spill in spills[2 * c : 2 * c + 2]:
-            spill.wait_recv()
-        extra, keep = ((high_in, keep_low), (low_in, keep_high))[c]
+            source, target, other = spill_low.at[k], low_in.at[k], down
+        spills[c] = remote(source, target, spill_send.at[c], spill_recv.at[c], in_ring(other))
+        spills[c].start()
+
+    for c in order:
+        spills[c].wait_recv()
+        extra, keep = (high_in, keep_low) if c < CHUNKS // 2 else (low_in, keep_high)
 
         @pl.loop(0, GROUPS)
         def _(q):
-            own[c, q] = own[c, q] + extra[q] * keep
+            own[c, q] = own[c, q] + extra[c % (CHUNKS // 2), q] * keep
 
         plane_exchange(
             lambda other: own.at[c, other], arrived.at[c, place], lines_send.at[c], lines_recv.at[c]
         )
         arrived[c, place] = own[c, place]
 
-    for c in range(CHUNKS):
+    for c in order:
         plane_wait(lines_recv.at[c])
         for p in range(PARTS):
             if p == 0 or p == PARTS - 1:
@@ -428,9 +454,9 @@
         ring_exchange(turned, stage_back, c, home_send, home_recv)
 
     def final(c):
-        return pl.ds(pl.multiple_of(RIM * c + ROWS * place, ROWS), ROWS)
-
-    for c in range(CHUNKS):
+        return pl.ds(pl.multiple_of(HOP // CHUNKS * c + ROWS * place, ROWS), ROWS)
+
+    for c in order:
         ring_wait(home_recv.at[c])
         plane_exchange(
             lambda other: stage_back.at[c, other], out.at[final(c)], last_send.at[c], last_recv.at[c]
@@ -444,14 +470,14 @@
             plane_wait(sem.at[c])
         for sem in (ring_send, home_send):
             ring_wait(sem.at[c])
-    for copy in halos + spills:
+    for copy in halos + list(spills.values()):
         copy.wait_send()
 
     @pl.when(tm == zed)
     def _():
         @pl.loop(1, RING)
         def _(step):
-            other = (tm + step) % RING
+            other = rem(tm + step, RING)
             remote(cuts_hbm, cuts, cut_send.at[step], cut_sem.at[0], {"tm": other}).wait_send()
 
 
@@ -459,8 +485,7 @@
     time, taper, chan, twist = tables()
     blocks = pltpu.VMEM((CHUNKS, GROUPS, ROWS, LANES), jnp.float32)
     half = pltpu.VMEM((CHUNKS, HALF, ROWS, LANES), jnp.float32)
-    rim = pltpu.VMEM((GROUPS, ROWS, LANES), jnp.float32)
-    sides = pltpu.VMEM((2, HOP, 2 * LANES), jnp.bfloat16)
+    rim = pltpu.VMEM((CHUNKS // 2, GROUPS, ROWS, LANES), jnp.float32)
     dma = pltpu.SemaphoreType.DMA
     return pl.pallas_call(
         body,
@@ -476,13 +501,11 @@
             blocks, blocks,
             pltpu.VMEM((PARTS, ROWS, 2 * LANES), jnp.float32),
             blocks, blocks, half, half,
-            pltpu.VMEM((2, HOP, LANES), jnp.int32),
-            sides, sides,
-            pltpu.VMEM((HOP, LANES), jnp.float32),
+            pltpu.VMEM((TIMES, 2 * LANES, LANES), jnp.int32),
+            pltpu.VMEM((TIMES, 2 * LANES, LANES), jnp.float32),
             blocks, rim, rim, rim, rim, blocks, blocks, blocks,
-            dma((9,)), dma((RING,)), dma((2,)),
-            dma((2,)), dma((2,)), dma((2,)), dma((2,)), dma((2,)), dma((2,)), dma((4,)), dma((4,)),
-            dma((4,)), dma((4,)), dma((2,)), dma((2,)), dma((2,)), dma((2,)), dma((2,)), dma((2,)),
+            dma((4 + CHUNKS,)), dma((RING,)), dma((2,)),
+            *[dma((CHUNKS,))] * 6, *[dma((2 * CHUNKS,))] * 2, *[dma((CHUNKS,))] * 8,
         ],
         compiler_params=pltpu.CompilerParams(
             collective_id=0, has_side_effects=True, vmem_limit_bytes=60 * 1024 * 1024

time: 120 us -> 110 us (0.917)
  Pallas kernels: 117 us -> 108 us
    pallas_call x1, Pallas kernels: 117 us -> 108 us  [per_device(): pl.pallas_call(body, out_shape=jax.ShapeDtypeStruct(record.shape, jnp.flo...]
where the time goes in v2:
time: 110 us
  Pallas kernels  108 us (98%)
  local copies, waits for them, and re-layouts  1.87 us (2%)
    pallas_call x1, Pallas kernels, per_device(): pl.pallas_call(body, out_shape=jax.ShapeDtypeStruct(record.shape, jnp.flo...  108 us

profile of v2, /device:TPU:1, one launch (start us, length us, event | category | flops | bytes accessed | tf_op | source)
XLA Modules:
  0.0 110.1 jit_solution(18233494251799454325)
XLA Ops:
  0.0 108.2 %shard_map.64 = f32[1024,128]{1,0:T(8,128)} custom-call(f32[1024,128]{1,0:T(8,128)} %record_hbm.1, s32[1,1024]{1,0:T(1,128)} %cuts_hbm.1, bf16[2,2,8,256,256]{4,3,2,1,0:T(8,128)(2,1)} %constant.8.clone.time_hbm, f32[2048,128]{1,0:T(8,128)} %constant.9.clone.taper_hbm, bf16[4,256,256]{2,1,0:T(8,128)(2,1)} %constant.10.clone.chan_hbm, ...), custom_call_target="tpu_custom_call" | custom-call | tf_op jit(solution)/shard_map/pallas_call | solution.py:490
  108.2 1.9 %copy.8 = f32[1024,128]{1,0:T(8,128)} copy(f32[1024,128]{1,0:T(8,128)} %shard_map.64) | data formatting | bytes 1048576

commit v3 on v2

--- a/solution.py
+++ b/solution.py
@@ -53,6 +53,7 @@
             blocks.append(np.block([[cosine, sine], [-sine, cosine]]))
     blocks = np.stack(blocks)
     time = np.stack([split_bf16(blocks), split_bf16(blocks.transpose(0, 2, 1))])
+    time = time.transpose(0, 2, 1, 3, 4).reshape(2, TIMES, 4 * LANES, 2 * LANES)
     taper = np.sin(np.pi / WIN * np.arange(WIN)) ** 2
     taper = np.repeat(taper[:, None], LANES, axis=1).astype(np.float32)
     lane = np.arange(LANES)
@@ -281,46 +282,14 @@
         load.wait()
 
     whole = 2 * LANES
-    for c in range(CHUNKS):
-        ring_wait(ring_recv.at[c])
-
-        @pl.loop(0, ROWS // 8)
-        def _(i):
-            rows = pl.ds(pl.multiple_of(i * 8, 8), 8)
-            lines = real_dft([recv[c, d, rows] for d in range(GROUPS)])
-            for p, (re, im) in enumerate(lines):
-                if p == 0:
-                    spec[p, rows, 0:LANES] = re
-                    spec[p, rows, LANES:whole] = jnp.zeros_like(re)
-                elif im is None:
-                    spec[p, rows, 0:LANES] = re * twist[0, p]
-                    spec[p, rows, LANES:whole] = -(re * twist[1, p])
-                else:
-                    cosine, sine = twist[0, p], twist[1, p]
-                    spec[p, rows, 0:LANES] = re * cosine + im * sine
-                    spec[p, rows, LANES:whole] = im * cosine - re * sine
-
-        lines = spec[...].reshape(PARTS * ROWS, whole)
-        lines = table_product(lines, chan[0], chan[1]).reshape(PARTS, ROWS, whole)
-        for p in range(PARTS):
-            re, im = lines[p, :, 0:LANES], lines[p, :, LANES:whole]
-            if p == 0:
-                coef[c, 0] = re - im
-            elif p == PARTS - 1:
-                coef[c, GROUPS - 1] = re - im
-            else:
-                coef[c, 2 * p - 1] = re
-                coef[c, 2 * p] = im
-
-        plane_exchange(
-            lambda other: coef.at[c, other], block.at[c, place], wave_send.at[c], wave_recv.at[c]
-        )
-        block[c, place] = coef[c, place]
+    keep_low = jnp.where(zed > 0, 1.0, 0.0).astype(jnp.float32)
+    keep_high = jnp.where(zed < RING - 1, 1.0, 0.0).astype(jnp.float32)
 
     halos = []
-    for c in range(CHUNKS):
+
+    def start_halo(c):
         plane_wait(wave_recv.at[c])
-        halos += [
+        halos.extend([
             remote(
                 block.at[c, pl.ds(HALF, HALF)], below.at[c],
                 halo_send.at[2 * c], halo_recv.at[2 * c], in_ring(up),
@@ -329,15 +298,13 @@
                 block.at[c, pl.ds(0, HALF)], above.at[c],
                 halo_send.at[2 * c + 1], halo_recv.at[2 * c + 1], in_ring(down),
             ),
-        ]
+        ])
         for halo in halos[-2:]:
             halo.start()
 
-    keep_low = jnp.where(zed > 0, 1.0, 0.0).astype(jnp.float32)
-    keep_high = jnp.where(zed < RING - 1, 1.0, 0.0).astype(jnp.float32)
-
     quarter = TALL // 4
-    for c in range(CHUNKS):
+
+    def fold(c):
         for halo in halos[2 * c : 2 * c + 2]:
             halo.wait_recv()
 
@@ -363,14 +330,59 @@
                     if p > 0:
                         lines_time[p, there] = im
 
+    for c in range(CHUNKS):
+        ring_wait(ring_recv.at[c])
+
+        @pl.loop(0, ROWS // 8)
+        def _(i):
+            rows = pl.ds(pl.multiple_of(i * 8, 8), 8)
+            lines = real_dft([recv[c, d, rows] for d in range(GROUPS)])
+            for p, (re, im) in enumerate(lines):
+                if p == 0:
+                    spec[p, rows, 0:LANES] = re
+                    spec[p, rows, LANES:whole] = jnp.zeros_like(re)
+                elif im is None:
+                    spec[p, rows, 0:LANES] = re * twist[0, p]
+                    spec[p, rows, LANES:whole] = -(re * twist[1, p])
+                else:
+                    cosine, sine = twist[0, p], twist[1, p]
+                    spec[p, rows, 0:LANES] = re * cosine + im * sine
+                    spec[p, rows, LANES:whole] = im * cosine - re * sine
+
+        lines = spec[...].reshape(PARTS * ROWS, whole)
+        lines = table_product(lines, chan[0], chan[1]).reshape(PARTS, ROWS, whole)
+        for p in range(PARTS):
+            re, im = lines[p, :, 0:LANES], lines[p, :, LANES:whole]
+            if p == 0:
+                coef[c, 0] = re - im
+            elif p == PARTS - 1:
+                coef[c, GROUPS - 1] = re - im
+            else:
+                coef[c, 2 * p - 1] = re
+                coef[c, 2 * p] = im
+
+        plane_exchange(
+            lambda other: coef.at[c, other], block.at[c, place], wave_send.at[c], wave_recv.at[c]
+        )
+        block[c, place] = coef[c, place]
+        if c > 0:
+            start_halo(c - 1)
+        if c > 1:
+            fold(c - 2)
+
+    start_halo(CHUNKS - 1)
+    fold(CHUNKS - 2)
+    fold(CHUNKS - 1)
+
     lane = lax.broadcasted_iota(jnp.int32, (1, LANES), 1)
     wave = div(place + 1, 2) + GROUPS * lane
     wave = jnp.minimum(wave, NCH - wave)
 
     def time_product(way, p, values):
         high, low = halves(values)
-        wide = dot(time[way, 0, p], jnp.concatenate([high, low], axis=1))
-        return wide[:, 0:LANES] + wide[:, LANES:whole] + dot(time[way, 1, p], high)
+        wide = dot(time[way, p], jnp.concatenate([high, low], axis=1))
+        main, rest = wide[0:whole], wide[whole : 2 * whole]
+        return (main[:, LANES:whole] + rest[:, 0:LANES]) + (rest[:, LANES:whole] + main[:, 0:LANES])
 
     for p in range(TIMES):
         values = time_product(0, p, lines_time[p])
@@ -409,7 +421,7 @@
         spills[c] = remote(source, target, spill_send.at[c], spill_recv.at[c], in_ring(other))
         spills[c].start()
 
-    for c in order:
+    def send_lines(c):
         spills[c].wait_recv()
         extra, keep = (high_in, keep_low) if c < CHUNKS // 2 else (low_in, keep_high)
 
@@ -422,7 +434,10 @@
         )
         arrived[c, place] = own[c, place]
 
-    for c in order:
+    send_lines(order[0])
+    for step, c in enumerate(order):
+        if step + 1 < CHUNKS:
+            send_lines(order[step + 1])
         plane_wait(lines_recv.at[c])
         for p in range(PARTS):
             if p == 0 or p == PARTS - 1:

time: 110 us -> 109 us (level)
  no operation moved by 1% of the time
where the time goes in v3:
time: 109 us
  Pallas kernels  107 us (98%)
  local copies, waits for them, and re-layouts  1.87 us (2%)
    pallas_call x1, Pallas kernels, per_device(): pl.pallas_call(body, out_shape=jax.ShapeDtypeStruct(record.shape, jnp.flo...  107 us

profile of v3, /device:TPU:1, one launch (start us, length us, event | category | flops | bytes accessed | tf_op | source)
XLA Modules:
  0.0 109.3 jit_solution(15877526540719295691)
XLA Ops:
  0.0 107.4 %shard_map.64 = f32[1024,128]{1,0:T(8,128)} custom-call(f32[1024,128]{1,0:T(8,128)} %record_hbm.1, s32[1,1024]{1,0:T(1,128)} %cuts_hbm.1, bf16[2,8,512,256]{3,2,1,0:T(8,128)(2,1)} %constant.8.clone.time_hbm, f32[2048,128]{1,0:T(8,128)} %constant.9.clone.taper_hbm, bf16[4,256,256]{2,1,0:T(8,128)(2,1)} %constant.10.clone.chan_hbm, ...), custom_call_target="tpu_custom_call" | custom-call | tf_op jit(solution)/shard_map/pallas_call | solution.py:505
  107.4 1.9 %copy.8 = f32[1024,128]{1,0:T(8,128)} copy(f32[1024,128]{1,0:T(8,128)} %shard_map.64) | data formatting | bytes 1048576

commit v4 on v3

--- a/solution.py
+++ b/solution.py
@@ -236,10 +236,12 @@
     def ring_wait(sem):
         bytes_of(recv, GROUPS - 2, sem).wait()
 
-    for c in range(CHUNKS):
+    def send_rows(c):
         plane_exchange(
             lambda other: piece(other, c), stage.at[c, place], rows_send.at[c], rows_recv.at[c]
         )
+
+    send_rows(0)
 
     @pl.when(tm == zed)
     def _():
@@ -253,6 +255,8 @@
         copy.wait()
 
     for c in range(CHUNKS):
+        if c + 1 < CHUNKS:
+            send_rows(c + 1)
         mine[c].wait()
         plane_wait(rows_recv.at[c])
         ring_exchange(stage, recv, c, ring_send, ring_recv)
@@ -388,7 +392,6 @@
         values = time_product(0, p, lines_time[p])
         lines_time[p] = time_product(1, p, jnp.where(wave <= limit[p], values, 0.0))
 
-    scale = 1.0 / (WIN * NCH)
     per = LANES // ROWS
 
     @pl.loop(0, per)
@@ -401,7 +404,7 @@
         lines.append((lines_time[0, there], None))
         for i, value in enumerate(real_inverse(lines)):
             weight = taper[pl.ds(pl.multiple_of(LANES * i + ROWS * g, ROWS), ROWS)]
-            value = value * (weight * scale)
+            value = value * weight
             if i < quarter:
                 target, k = spill_low, i
             elif i < 3 * quarter:
@@ -502,7 +505,7 @@
     half = pltpu.VMEM((CHUNKS, HALF, ROWS, LANES), jnp.float32)
     rim = pltpu.VMEM((CHUNKS // 2, GROUPS, ROWS, LANES), jnp.float32)
     dma = pltpu.SemaphoreType.DMA
-    return pl.pallas_call(
+    result = pl.pallas_call(
         body,
         out_shape=jax.ShapeDtypeStruct(record.shape, jnp.float32),
         in_specs=[pl.BlockSpec(memory_space=pltpu.HBM)] * 6,
@@ -526,6 +529,7 @@
             collective_id=0, has_side_effects=True, vmem_limit_bytes=60 * 1024 * 1024
         ),
     )(record, cuts, time, taper, chan, twist)
+    return result * (1.0 / (WIN * NCH))
 
 
 def solution(mesh):

time: 109 us -> 109 us (level)
  other arithmetic: 0 us -> 1.87 us
  local copies, waits for them, and re-layouts: 1.87 us -> 0 us
    mul x0 -> x1, other arithmetic: none -> 1.87 us  [per_device(): return result * (1.0 / (WIN * NCH))]
    unnamed x1 -> x0, local copies, waits for them, and re-layouts: 1.87 us -> none
where the time goes in v4:
time: 109 us
  Pallas kernels  107 us (98%)
  other arithmetic  1.87 us (2%)
    pallas_call x1, Pallas kernels, per_device(): pl.pallas_call(body, out_shape=jax.ShapeDtypeStruct(record.shape, jnp.flo...  107 us

profile of v4, /device:TPU:1, one launch (start us, length us, event | category | flops | bytes accessed | tf_op | source)
XLA Modules:
  0.0 108.7 jit_solution(5202033580353778656)
XLA Ops:
  0.0 106.8 %shard_map.64 = f32[1024,128]{1,0:T(8,128)} custom-call(f32[1024,128]{1,0:T(8,128)} %record_hbm.1, s32[1,1024]{1,0:T(1,128)} %cuts_hbm.1, bf16[2,8,512,256]{3,2,1,0:T(8,128)(2,1)} %constant.10.clone.time_hbm, f32[2048,128]{1,0:T(8,128)} %constant.11.clone.taper_hbm, bf16[4,256,256]{2,1,0:T(8,128)(2,1)} %constant.12.clone.chan_hbm, ...), custom_call_target="tpu_custom_call" | custom-call | tf_op jit(solution)/shard_map/pallas_call | solution.py:508
  106.8 1.9 %broadcast_multiply_fusion = f32[1024,128]{1,0:T(8,128)} fusion(f32[1024,128]{1,0:T(8,128)} %shard_map.64), kind=kLoop, calls=%fused_computation | loop fusion | flops 131072 | bytes 1048576 | tf_op jit(solution)/shard_map/mul | solution.py:532

commit v5 on v4

--- a/solution.py
+++ b/solution.py
@@ -187,14 +187,12 @@
 
     barrier = pltpu.get_barrier_semaphore()
 
-    @pl.loop(1, GROUPS)
-    def _(step):
-        other = rem(place + 11 * step, GROUPS)
+    for step in range(1, GROUPS):
+        other = rem(place + 11 * step % GROUPS, GROUPS)
         pl.semaphore_signal(barrier, inc=1, device_id=in_plane(other), device_id_type=MESH_ID)
 
-    @pl.loop(1, RING)
-    def _(step):
-        other = rem(zed + 7 * step, RING)
+    for step in range(1, RING):
+        other = rem(zed + 7 * step % RING, RING)
         pl.semaphore_signal(barrier, inc=1, device_id=in_ring(other), device_id_type=MESH_ID)
 
     for load in mine + loads:
@@ -209,15 +207,13 @@
         )
 
     def plane_exchange(source_of, target, send_sem, recv_sem):
-        @pl.loop(1, GROUPS)
-        def _(step):
-            other = rem(place + 11 * step, GROUPS)
+        for step in range(1, GROUPS):
+            other = rem(place + 11 * step % GROUPS, GROUPS)
             remote(source_of(other), target, send_sem, recv_sem, in_plane(other)).start()
 
     def ring_exchange(source, target, chunk, send_sem, recv_sem):
-        @pl.loop(1, RING)
-        def _(step):
-            other = rem(zed + 7 * step, RING)
+        for step in range(1, RING):
+            other = rem(zed + 7 * step % RING, RING)
             remote(
                 source.at[chunk, pl.ds(2 * other, 2)], target.at[chunk, pl.ds(2 * zed, 2)],
                 send_sem.at[chunk], recv_sem.at[chunk], in_ring(other),

time: 109 us -> 108 us (level)
  no operation moved by 1% of the time
where the time goes in v5:
time: 108 us
  Pallas kernels  106 us (98%)
  other arithmetic  1.87 us (2%)
    pallas_call x1, Pallas kernels, per_device(): pl.pallas_call(body, out_shape=jax.ShapeDtypeStruct(record.shape, jnp.flo...  106 us

profile of v5, /device:TPU:1, one launch (start us, length us, event | category | flops | bytes accessed | tf_op | source)
XLA Modules:
  0.0 108.3 jit_solution(14422509318141799046)
XLA Ops:
  0.0 106.4 %shard_map.64 = f32[1024,128]{1,0:T(8,128)} custom-call(f32[1024,128]{1,0:T(8,128)} %record_hbm.1, s32[1,1024]{1,0:T(1,128)} %cuts_hbm.1, bf16[2,8,512,256]{3,2,1,0:T(8,128)(2,1)} %constant.10.clone.time_hbm, f32[2048,128]{1,0:T(8,128)} %constant.11.clone.taper_hbm, bf16[4,256,256]{2,1,0:T(8,128)(2,1)} %constant.12.clone.chan_hbm, ...), custom_call_target="tpu_custom_call" | custom-call | tf_op jit(solution)/shard_map/pallas_call | solution.py:504
  106.4 1.9 %broadcast_multiply_fusion = f32[1024,128]{1,0:T(8,128)} fusion(f32[1024,128]{1,0:T(8,128)} %shard_map.64), kind=kLoop, calls=%fused_computation | loop fusion | flops 131072 | bytes 1048576 | tf_op jit(solution)/shard_map/mul | solution.py:528

commit v6 on v5

--- a/solution.py
+++ b/solution.py
@@ -250,12 +250,17 @@
         copy.start()
         copy.wait()
 
-    for c in range(CHUNKS):
+    def send_ring(c):
+        mine[c].wait()
+        plane_wait(rows_recv.at[c])
+        if c > 1:
+            ring_wait(ring_recv.at[c - 2])
+        ring_exchange(stage, recv, c, ring_send, ring_recv)
         if c + 1 < CHUNKS:
             send_rows(c + 1)
-        mine[c].wait()
-        plane_wait(rows_recv.at[c])
-        ring_exchange(stage, recv, c, ring_send, ring_recv)
+
+    send_ring(0)
+    send_ring(1)
 
     @pl.when(tm != zed)
     def _():
@@ -331,7 +336,10 @@
                         lines_time[p, there] = im
 
     for c in range(CHUNKS):
-        ring_wait(ring_recv.at[c])
+        if c + 2 < CHUNKS:
+            send_ring(c + 2)
+        else:
+            ring_wait(ring_recv.at[c])
 
         @pl.loop(0, ROWS // 8)
         def _(i):
@@ -418,10 +426,14 @@
         else:
             source, target, other = spill_low.at[k], low_in.at[k], down
         spills[c] = remote(source, target, spill_send.at[c], spill_recv.at[c], in_ring(other))
+    for c in order[:2]:
         spills[c].start()
 
     def send_lines(c):
         spills[c].wait_recv()
+        if c == order[0]:
+            for later in order[2:]:
+                spills[later].start()
         extra, keep = (high_in, keep_low) if c < CHUNKS // 2 else (low_in, keep_high)
 
         @pl.loop(0, GROUPS)
@@ -433,11 +445,18 @@
         )
         arrived[c, place] = own[c, place]
 
+    def send_home(c):
+        final = pl.ds(pl.multiple_of(HOP // CHUNKS * c + ROWS * place, ROWS), ROWS)
+        plane_exchange(
+            lambda other: stage_back.at[c, other], out.at[final], last_send.at[c], last_recv.at[c]
+        )
+        out[final] = stage_back[c, place]
+
     send_lines(order[0])
     for step, c in enumerate(order):
+        plane_wait(lines_recv.at[c])
         if step + 1 < CHUNKS:
             send_lines(order[step + 1])
-        plane_wait(lines_recv.at[c])
         for p in range(PARTS):
             if p == 0 or p == PARTS - 1:
                 re = arrived[c, 0 if p == 0 else GROUPS - 1]
@@ -465,17 +484,15 @@
             for d, value in enumerate(real_inverse(lines)):
                 turned[c, d, rows] = value
 
+        if step > 1:
+            ring_wait(home_recv.at[order[step - 2]])
         ring_exchange(turned, stage_back, c, home_send, home_recv)
-
-    def final(c):
-        return pl.ds(pl.multiple_of(HOP // CHUNKS * c + ROWS * place, ROWS), ROWS)
-
-    for c in order:
+        if step > 1:
+            send_home(order[step - 2])
+
+    for c in order[-2:]:
         ring_wait(home_recv.at[c])
-        plane_exchange(
-            lambda other: stage_back.at[c, other], out.at[final(c)], last_send.at[c], last_recv.at[c]
-        )
-        out[final(c)] = stage_back[c, place]
+        send_home(c)
 
     for c in range(CHUNKS):
         plane_wait(last_recv.at[c])

time: 108 us -> 110 us (1.019)
  Pallas kernels: 106 us -> 108 us
    pallas_call x1, Pallas kernels: 106 us -> 108 us  [per_device(): pl.pallas_call(body, out_shape=jax.ShapeDtypeStruct(record.shape, jnp.flo...]
where the time goes in v6:
time: 110 us
  Pallas kernels  108 us (98%)
  other arithmetic  1.87 us (2%)
    pallas_call x1, Pallas kernels, per_device(): pl.pallas_call(body, out_shape=jax.ShapeDtypeStruct(record.shape, jnp.flo...  108 us

profile of v6, /device:TPU:1, one launch (start us, length us, event | category | flops | bytes accessed | tf_op | source)
XLA Modules:
  0.0 110.2 jit_solution(17491909645769187775)
XLA Ops:
  0.0 108.3 %shard_map.64 = f32[1024,128]{1,0:T(8,128)} custom-call(f32[1024,128]{1,0:T(8,128)} %record_hbm.1, s32[1,1024]{1,0:T(1,128)} %cuts_hbm.1, bf16[2,8,512,256]{3,2,1,0:T(8,128)(2,1)} %constant.10.clone.time_hbm, f32[2048,128]{1,0:T(8,128)} %constant.11.clone.taper_hbm, bf16[4,256,256]{2,1,0:T(8,128)(2,1)} %constant.12.clone.chan_hbm, ...), custom_call_target="tpu_custom_call" | custom-call | tf_op jit(solution)/shard_map/pallas_call | solution.py:521
  108.3 1.9 %broadcast_multiply_fusion = f32[1024,128]{1,0:T(8,128)} fusion(f32[1024,128]{1,0:T(8,128)} %shard_map.64), kind=kLoop, calls=%fused_computation | loop fusion | flops 131072 | bytes 1048576 | tf_op jit(solution)/shard_map/mul | solution.py:545

commit v7 on v5

--- a/solution.py
+++ b/solution.py
@@ -150,10 +150,10 @@
     record_hbm, cuts_hbm, time_hbm, taper_hbm, chan_hbm, twist_hbm,
     out,
     cuts, time, taper, chan, twist,
-    stage, recv, spec, coef, block, below, above, limit, lines_time,
+    recv, spec, coef, block, below, above, limit, lines_time,
     own, spill_low, spill_high, low_in, high_in, arrived, turned, stage_back,
     load_sem, cut_send, cut_sem,
-    rows_send, rows_recv, ring_send, ring_recv, wave_send, wave_recv, halo_send, halo_recv,
+    rows_send, ring_recv, wave_send, wave_recv, halo_send, halo_recv,
     spill_send, spill_recv, lines_send, lines_recv, home_send, home_recv, last_send, last_recv,
 ):
     tm = lax.axis_index("tm")
@@ -180,11 +180,6 @@
     def piece(other, chunk):
         return record_hbm.at[pl.ds(pl.multiple_of(32 * other + ROWS * chunk, ROWS), ROWS)]
 
-    mine = [
-        pltpu.make_async_copy(piece(place, c), stage.at[c, place], load_sem.at[4 + c])
-        for c in range(CHUNKS)
-    ]
-
     barrier = pltpu.get_barrier_semaphore()
 
     for step in range(1, GROUPS):
@@ -195,10 +190,16 @@
         other = rem(zed + 7 * step % RING, RING)
         pl.semaphore_signal(barrier, inc=1, device_id=in_ring(other), device_id_type=MESH_ID)
 
-    for load in mine + loads:
+    @pl.loop(0, GROUPS)
+    def _(step):
+        pl.semaphore_signal(
+            barrier, inc=1, device_id={"tm": zed, "chan": step}, device_id_type=MESH_ID
+        )
+
+    for load in loads:
         load.start()
 
-    pl.semaphore_wait(barrier, GROUPS + RING - 2)
+    pl.semaphore_wait(barrier, 2 * GROUPS + RING - 2)
 
     def remote(source, target, send_sem, recv_sem, device):
         return pltpu.make_async_remote_copy(
@@ -232,12 +233,20 @@
     def ring_wait(sem):
         bytes_of(recv, GROUPS - 2, sem).wait()
 
-    def send_rows(c):
-        plane_exchange(
-            lambda other: piece(other, c), stage.at[c, place], rows_send.at[c], rows_recv.at[c]
-        )
-
-    send_rows(0)
+    for c in range(CHUNKS):
+        @pl.loop(0, GROUPS)
+        def _(step):
+            other = rem(place + 11 * step, GROUPS)
+            target = recv.at[c, chan_index]
+
+            @pl.when(jnp.logical_or(tm != zed, step != 0))
+            def _():
+                where = {"tm": div(other, 2), "chan": 2 * tm + rem(other, 2)}
+                remote(piece(other, c), target, rows_send.at[c], ring_recv.at[c], where).start()
+
+            @pl.when(jnp.logical_and(tm == zed, step == 0))
+            def _():
+                pltpu.make_async_copy(piece(other, c), target, ring_recv.at[c]).start()
 
     @pl.when(tm == zed)
     def _():
@@ -249,13 +258,6 @@
         copy = pltpu.make_async_copy(cuts_hbm, cuts, cut_sem.at[1])
         copy.start()
         copy.wait()
-
-    for c in range(CHUNKS):
-        if c + 1 < CHUNKS:
-            send_rows(c + 1)
-        mine[c].wait()
-        plane_wait(rows_recv.at[c])
-        ring_exchange(stage, recv, c, ring_send, ring_recv)
 
     @pl.when(tm != zed)
     def _():
@@ -331,7 +333,7 @@
                         lines_time[p, there] = im
 
     for c in range(CHUNKS):
-        ring_wait(ring_recv.at[c])
+        bytes_of(recv, GROUPS, ring_recv.at[c]).wait()
 
         @pl.loop(0, ROWS // 8)
         def _(i):
@@ -480,10 +482,17 @@
     for c in range(CHUNKS):
         plane_wait(last_recv.at[c])
     for c in range(CHUNKS):
-        for sem in (rows_send, wave_send, lines_send, last_send):
+        for sem in (wave_send, lines_send, last_send):
             plane_wait(sem.at[c])
-        for sem in (ring_send, home_send):
-            ring_wait(sem.at[c])
+        ring_wait(home_send.at[c])
+
+        @pl.when(tm == zed)
+        def _():
+            bytes_of(recv, GROUPS - 1, rows_send.at[c]).wait()
+
+        @pl.when(tm != zed)
+        def _():
+            bytes_of(recv, GROUPS, rows_send.at[c]).wait()
     for copy in halos + list(spills.values()):
         copy.wait_send()
 
@@ -512,14 +521,14 @@
             pltpu.VMEM(taper.shape, jnp.float32),
             pltpu.VMEM(chan.shape, jnp.bfloat16),
             pltpu.VMEM(twist.shape, jnp.float32),
-            blocks, blocks,
+            blocks,
             pltpu.VMEM((PARTS, ROWS, 2 * LANES), jnp.float32),
             blocks, blocks, half, half,
             pltpu.VMEM((TIMES, 2 * LANES, LANES), jnp.int32),
             pltpu.VMEM((TIMES, 2 * LANES, LANES), jnp.float32),
             blocks, rim, rim, rim, rim, blocks, blocks, blocks,
-            dma((4 + CHUNKS,)), dma((RING,)), dma((2,)),
-            *[dma((CHUNKS,))] * 6, *[dma((2 * CHUNKS,))] * 2, *[dma((CHUNKS,))] * 8,
+            dma((4,)), dma((RING,)), dma((2,)),
+            *[dma((CHUNKS,))] * 4, *[dma((2 * CHUNKS,))] * 2, *[dma((CHUNKS,))] * 8,
         ],
         compiler_params=pltpu.CompilerParams(
             collective_id=0, has_side_effects=True, vmem_limit_bytes=60 * 1024 * 1024

time: 108 us -> 161 us (1.49)
  Pallas kernels: 106 us -> 159 us
    pallas_call x1, Pallas kernels: 106 us -> 159 us  [per_device(): pl.pallas_call(body, out_shape=jax.ShapeDtypeStruct(record.shape, jnp.flo...]
where the time goes in v7:
time: 161 us; the launch traced here: 160 us
  Pallas kernels  159 us (99%)
  other arithmetic  1.87 us (1%)
    pallas_call x1, Pallas kernels, per_device(): pl.pallas_call(body, out_shape=jax.ShapeDtypeStruct(record.shape, jnp.flo...  159 us

profile of v7, /device:TPU:1, one launch (start us, length us, event | category | flops | bytes accessed | tf_op | source)
XLA Modules:
  0.0 160.4 jit_solution(3709450146836725913)
XLA Ops:
  0.0 158.6 %shard_map.64 = f32[1024,128]{1,0:T(8,128)} custom-call(f32[1024,128]{1,0:T(8,128)} %record_hbm.1, s32[1,1024]{1,0:T(1,128)} %cuts_hbm.1, bf16[2,8,512,256]{3,2,1,0:T(8,128)(2,1)} %constant.10.clone.time_hbm, f32[2048,128]{1,0:T(8,128)} %constant.11.clone.taper_hbm, bf16[4,256,256]{2,1,0:T(8,128)(2,1)} %constant.12.clone.chan_hbm, ...), custom_call_target="tpu_custom_call" | custom-call | tf_op jit(solution)/shard_map/pallas_call | solution.py:513
  158.6 1.9 %broadcast_multiply_fusion = f32[1024,128]{1,0:T(8,128)} fusion(f32[1024,128]{1,0:T(8,128)} %shard_map.64), kind=kLoop, calls=%fused_computation | loop fusion | flops 131072 | bytes 1048576 | tf_op jit(solution)/shard_map/mul | solution.py:537

commit v8 on v5

--- a/solution.py
+++ b/solution.py
@@ -151,10 +151,10 @@
     out,
     cuts, time, taper, chan, twist,
     stage, recv, spec, coef, block, below, above, limit, lines_time,
-    own, spill_low, spill_high, low_in, high_in, arrived, turned, stage_back,
+    own, spill_low, spill_high, low_in, high_in, arrived, turned,
     load_sem, cut_send, cut_sem,
     rows_send, rows_recv, ring_send, ring_recv, wave_send, wave_recv, halo_send, halo_recv,
-    spill_send, spill_recv, lines_send, lines_recv, home_send, home_recv, last_send, last_recv,
+    spill_send, spill_recv, lines_send, lines_recv, last_send, last_recv,
 ):
     tm = lax.axis_index("tm")
     chan_index = lax.axis_index("chan")
@@ -195,10 +195,15 @@
         other = rem(zed + 7 * step % RING, RING)
         pl.semaphore_signal(barrier, inc=1, device_id=in_ring(other), device_id_type=MESH_ID)
 
+    @pl.loop(0, GROUPS)
+    def _(step):
+        where = {"tm": div(step, 2), "chan": 2 * tm + rem(step, 2)}
+        pl.semaphore_signal(barrier, inc=1, device_id=where, device_id_type=MESH_ID)
+
     for load in mine + loads:
         load.start()
 
-    pl.semaphore_wait(barrier, GROUPS + RING - 2)
+    pl.semaphore_wait(barrier, 2 * GROUPS + RING - 2)
 
     def remote(source, target, send_sem, recv_sem, device):
         return pltpu.make_async_remote_copy(
@@ -465,25 +470,36 @@
             for d, value in enumerate(real_inverse(lines)):
                 turned[c, d, rows] = value
 
-        ring_exchange(turned, stage_back, c, home_send, home_recv)
-
-    def final(c):
-        return pl.ds(pl.multiple_of(HOP // CHUNKS * c + ROWS * place, ROWS), ROWS)
-
-    for c in order:
-        ring_wait(home_recv.at[c])
-        plane_exchange(
-            lambda other: stage_back.at[c, other], out.at[final(c)], last_send.at[c], last_recv.at[c]
-        )
-        out[final(c)] = stage_back[c, place]
+        final = pl.ds(pl.multiple_of(HOP // CHUNKS * c + ROWS * place, ROWS), ROWS)
+
+        @pl.loop(0, GROUPS)
+        def _(hop):
+            other = rem(chan_index + 11 * hop, GROUPS)
+            source, target = turned.at[c, other], out.at[final]
+
+            @pl.when(jnp.logical_or(tm != zed, hop != 0))
+            def _():
+                where = {"tm": zed, "chan": other}
+                remote(source, target, last_send.at[c], last_recv.at[c], where).start()
+
+            @pl.when(jnp.logical_and(tm == zed, hop == 0))
+            def _():
+                pltpu.make_async_copy(source, target, last_recv.at[c]).start()
 
     for c in range(CHUNKS):
-        plane_wait(last_recv.at[c])
+        bytes_of(recv, GROUPS, last_recv.at[c]).wait()
     for c in range(CHUNKS):
-        for sem in (rows_send, wave_send, lines_send, last_send):
+        for sem in (rows_send, wave_send, lines_send):
             plane_wait(sem.at[c])
-        for sem in (ring_send, home_send):
-            ring_wait(sem.at[c])
+        ring_wait(ring_send.at[c])
+
+        @pl.when(tm == zed)
+        def _():
+            bytes_of(recv, GROUPS - 1, last_send.at[c]).wait()
+
+        @pl.when(tm != zed)
+        def _():
+            bytes_of(recv, GROUPS, last_send.at[c]).wait()
     for copy in halos + list(spills.values()):
         copy.wait_send()
 
@@ -517,9 +533,9 @@
             blocks, blocks, half, half,
             pltpu.VMEM((TIMES, 2 * LANES, LANES), jnp.int32),
             pltpu.VMEM((TIMES, 2 * LANES, LANES), jnp.float32),
-            blocks, rim, rim, rim, rim, blocks, blocks, blocks,
+            blocks, rim, rim, rim, rim, blocks, blocks,
             dma((4 + CHUNKS,)), dma((RING,)), dma((2,)),
-            *[dma((CHUNKS,))] * 6, *[dma((2 * CHUNKS,))] * 2, *[dma((CHUNKS,))] * 8,
+            *[dma((CHUNKS,))] * 6, *[dma((2 * CHUNKS,))] * 2, *[dma((CHUNKS,))] * 6,
         ],
         compiler_params=pltpu.CompilerParams(
             collective_id=0, has_side_effects=True, vmem_limit_bytes=60 * 1024 * 1024

time: 108 us -> 107 us (level)
  the two profiles are of different devices: /device:TPU:1 before, /device:TPU:8 now
where the time goes in v8:
time: 107 us
  Pallas kernels  105 us (98%)
  other arithmetic  1.87 us (2%)
    pallas_call x1, Pallas kernels, per_device(): pl.pallas_call(body, out_shape=jax.ShapeDtypeStruct(record.shape, jnp.flo...  105 us

profile of v8, /device:TPU:8, one launch (start us, length us, event | category | flops | bytes accessed | tf_op | source)
XLA Modules:
  0.0 107.2 jit_solution(2750831278513091727)
XLA Ops:
  0.0 105.3 %shard_map.64 = f32[1024,128]{1,0:T(8,128)} custom-call(f32[1024,128]{1,0:T(8,128)} %record_hbm.1, s32[1,1024]{1,0:T(1,128)} %cuts_hbm.1, bf16[2,8,512,256]{3,2,1,0:T(8,128)(2,1)} %constant.10.clone.time_hbm, f32[2048,128]{1,0:T(8,128)} %constant.11.clone.taper_hbm, bf16[4,256,256]{2,1,0:T(8,128)(2,1)} %constant.12.clone.chan_hbm, ...), custom_call_target="tpu_custom_call" | custom-call | tf_op jit(solution)/shard_map/pallas_call | solution.py:520
  105.3 1.9 %broadcast_multiply_fusion = f32[1024,128]{1,0:T(8,128)} fusion(f32[1024,128]{1,0:T(8,128)} %shard_map.64), kind=kLoop, calls=%fused_computation | loop fusion | flops 131072 | bytes 1048576 | tf_op jit(solution)/shard_map/mul | solution.py:544
